TPU v7x, 32 devices: a whole 2x2x4 slice. The times are simulated.
32 devices in a mesh: section: 2 (over y), dp: 4 (over z), tensor: 4 (over x, core).
Axes of the slice: x: 2, y: 2, z: 4, core: 2. Of those that a mesh axis runs over, the one named last changes fastest.
Arguments:
- inputs: bfloat16 [4, 2048, 768], P(None, ('dp', 'tensor')), may hold values from -6 to 6
- cotangent: bfloat16 [4, 2048, 768], P(None, ('dp', 'tensor')), may hold values from -6 to 6
- seq_lengths: int32 [4, 4, 4], P('dp'), may hold values from 0 to 512, as said below
- w_attn: bfloat16 [2, 768, 3, 768], P('section', None, None, 'tensor'), may hold values from -0.21875 to 0.21875
- b_qv: bfloat16 [2, 2, 768], P('section', None, 'tensor'), may hold values from -3 to 3
- w_proj: bfloat16 [2, 768, 768], P('section', 'tensor'), may hold values from -0.875 to 0.875
- b_proj: bfloat16 [2, 768], P('section'), may hold values from -3 to 3
- w_fc: bfloat16 [2, 768, 3072], P('section', None, 'tensor'), may hold values from -0.21875 to 0.21875
- b_fc: bfloat16 [2, 3072], P('section', 'tensor'), may hold values from -3 to 3
- w_out: bfloat16 [2, 3072, 768], P('section', 'tensor'), may hold values from -0.109375 to 0.109375
- b_out: bfloat16 [2, 768], P('section'), may hold values from -3 to 3
- ln_gain: bfloat16 [2, 2, 768], P('section'), may hold values from 0.25 to 1.75
- ln_bias: bfloat16 [2, 2, 768], P('section'), may hold values from -2 to 2
Outputs:
- section_out: bfloat16 [2, 4, 2048, 768], P('section', None, ('dp', 'tensor'))
- input_grad: bfloat16 [2, 4, 2048, 768], P('section', None, ('dp', 'tensor'))
- grad_w_attn: float32 [2, 768, 3, 768], P('section', 'dp', None, 'tensor')
- grad_b_qv: float32 [2, 2, 768], P('section', None, 'tensor')
- grad_w_proj: float32 [2, 768, 768], P('section', 'tensor', 'dp')
- grad_b_proj: float32 [2, 768], P('section', ('dp', 'tensor'))
- grad_w_fc: float32 [2, 768, 3072], P('section', 'dp', 'tensor')
- grad_b_fc: float32 [2, 3072], P('section', 'tensor')
- grad_w_out: float32 [2, 3072, 768], P('section', 'tensor', 'dp')
- grad_b_out: float32 [2, 768], P('section', ('dp', 'tensor'))
- grad_ln_gain: float32 [2, 2, 768], P('section', None, ('dp', 'tensor'))
- grad_ln_bias: float32 [2, 2, 768], P('section', None, ('dp', 'tensor'))
Inputs may be any that keep to these rules, and one draw needn't show every extreme that they name: seq_lengths[g, m, j] is the number of slots of the j-th sequence of micro-batch m on data group g; the sequences lie end to end from slot 0 and slots after them are padding; each (g, m) totals at most 512, and on every group some micro-batch is one sequence of 512 slots.
All inputs are finite; a program needn't handle non-finite values.
Results may differ from a plain program's by a relative error of at most 0.02.
Values may be sent and summed in bfloat16 or wider, within the bound.
No kernel may reach another device: no remote copies, remote signals or barrier semaphores. Data moves between devices by JAX's collectives and lax.ppermute only.
A program may use at most 128 MiB of HBM per device.

v0:
```python
import jax
import jax.numpy as jnp
from jax import lax
from jax.sharding import PartitionSpec as P

HEAD_DIM = 64


def shifted(block, axis, distance):
    devices = range(lax.axis_size(axis))
    route = [(i - distance, i) for i in devices if i - distance in devices]
    return lax.ppermute(block, axis, route)


def layer_norm(rows, gain, shift):
    center = jnp.mean(rows, axis=-1, keepdims=True)
    centred = rows - center
    variance = jnp.mean(centred * centred, axis=-1, keepdims=True)
    return centred * lax.rsqrt(variance + 1e-05) * gain + shift


def gelu_tanh(values):
    return jax.nn.gelu(values, approximate=True)


def inner(left, right):
    return lax.dot_general(
        left, right, (((0,), (0,)), ((), ())), preferred_element_type=jnp.float32
    )


def by_transpose(left, right):
    return lax.dot_general(
        left, right, (((1,), (1,)), ((), ())), preferred_element_type=jnp.float32
    )


def masks_for(lengths, total_rows, own_start, own_rows):
    ends = jnp.cumsum(lengths)
    position = jnp.arange(total_rows, dtype=jnp.int32)
    segment = jnp.sum((position[:, None] >= ends[None, :]).astype(jnp.int32), axis=1)
    own = lax.dynamic_slice_in_dim(position, own_start, own_rows)
    live = (own < ends[-1]).astype(jnp.float32)[:, None]
    return (segment, live)


def gather_rows(normed):
    return lax.all_gather(normed, "tensor", axis=0, tiled=True)


def gather_grads(grads):
    return lax.all_gather(grads, "tensor", axis=0, tiled=True)


def row_sum(left, weight):
    return lax.psum_scatter(
        jnp.dot(left, weight, preferred_element_type=jnp.float32).astype(jnp.bfloat16),
        "tensor",
        scatter_dimension=0,
        tiled=True,
    ).astype(jnp.float32)


def grad_sum(left, weight):
    return lax.psum_scatter(
        by_transpose(left, weight).astype(jnp.bfloat16), "tensor", scatter_dimension=0, tiled=True
    ).astype(jnp.float32)


def block_scores(queries, keys, segment, start, span, scale):
    total = keys.shape[0]
    position = jnp.arange(total, dtype=jnp.int32)
    pos_block = start + jnp.arange(span, dtype=jnp.int32)
    allowed = (segment[:, None] == segment[None, :]) & (position[None, :] <= pos_block[:, None])
    scores = jnp.einsum("qhd,khd->hqk", queries, keys, preferred_element_type=jnp.float32) * scale
    return (jnp.where(allowed[None], scores, -1e30), queries)


def attend_forward(queries, keys, values, segment, scale):
    total = queries.shape[0]
    span = min(512, total)

    def one(index):
        start = index * span
        scores, unused = block_scores(queries, keys, segment, start, span, scale)
        top = jnp.max(scores, axis=-1, keepdims=True)
        expo = jnp.exp(scores - top)
        norm_total = jnp.sum(expo, axis=-1, keepdims=True)
        weights = (expo / norm_total).astype(jnp.bfloat16)
        context = jnp.einsum("hqk,khd->qhd", weights, values, preferred_element_type=jnp.float32)
        return (context, (top + jnp.log(norm_total))[..., 0])

    context, logsum = lax.map(one, jnp.arange(total // span))
    return (context.reshape(total, -1), logsum)


def attend_backward(queries, keys, values, segment, logsum, grad_context, scale):
    total = queries.shape[0]
    span = min(512, total)

    def one(carry, index):
        grad_keys, grad_values = carry
        start = index * span
        scores, query_block = block_scores(queries, keys, segment, start, span, scale)
        probs = jnp.exp(scores - logsum[index][:, :, None])
        weights = probs.astype(jnp.bfloat16)
        grad_values = grad_values + jnp.einsum(
            "hqk,qhd->khd", weights, grad_context, preferred_element_type=jnp.float32
        )
        grad_probs = jnp.einsum(
            "qhd,khd->hqk", grad_context, values, preferred_element_type=jnp.float32
        )
        weighted = jnp.sum(probs * grad_probs, axis=-1, keepdims=True)
        grad_scores = (probs * (grad_probs - weighted)).astype(jnp.bfloat16)
        grad_query = (
            jnp.einsum("hqk,khd->qhd", grad_scores, keys, preferred_element_type=jnp.float32)
            * scale
        )
        grad_keys = (
            grad_keys
            + jnp.einsum(
                "hqk,qhd->khd", grad_scores, query_block, preferred_element_type=jnp.float32
            )
            * scale
        )
        return ((grad_keys, grad_values), grad_query)

    zeros = jnp.zeros(keys.shape, jnp.float32)
    (grad_keys, grad_values), grad_queries = lax.scan(
        one, (zeros, zeros), jnp.arange(total // span)
    )
    return (
        grad_queries.reshape(total, -1),
        grad_keys.reshape(total, -1),
        grad_values.reshape(total, -1),
    )


def forward_block(params, rows, segment, live, scale):
    w_attn, b_qv, w_proj, b_proj, w_fc, b_fc, w_out, b_out, ln_gain, ln_bias = params
    width = w_attn.shape[-1]
    normed_all = gather_rows(layer_norm(rows, ln_gain[0], ln_bias[0]).astype(jnp.bfloat16))
    total = normed_all.shape[0]
    mixed = jnp.dot(
        normed_all, w_attn.reshape(w_attn.shape[0], 3 * width), preferred_element_type=jnp.float32
    )
    bias_row = jnp.concatenate([b_qv[0], jnp.zeros_like(b_qv[0]), b_qv[1]])
    mixed = (mixed + bias_row).astype(jnp.bfloat16)
    heads = width // HEAD_DIM
    queries = mixed[:, :width].reshape(total, heads, HEAD_DIM)
    keys = mixed[:, width : 2 * width].reshape(total, heads, HEAD_DIM)
    values = mixed[:, 2 * width :].reshape(total, heads, HEAD_DIM)
    context, logsum = attend_forward(queries, keys, values, segment, scale)
    context = context.astype(jnp.bfloat16)
    middle = rows + (row_sum(context, w_proj) + b_proj)
    normed_two_all = gather_rows(layer_norm(middle, ln_gain[1], ln_bias[1]).astype(jnp.bfloat16))
    hidden = jnp.dot(normed_two_all, w_fc, preferred_element_type=jnp.float32) + b_fc
    active = gelu_tanh(hidden).astype(jnp.bfloat16)
    result = live * (middle + (row_sum(active, w_out) + b_out))
    kept = (rows, middle, normed_all, mixed, logsum, context, normed_two_all, hidden, active)
    return (result.astype(jnp.bfloat16), kept)


def backward_block(params, kept, grad_out, segment, live, scale):
    w_attn, b_qv, w_proj, b_proj, w_fc, b_fc, w_out, b_out, ln_gain, ln_bias = params
    rows, middle, normed_all, mixed, logsum, context, normed_two_all, hidden, active = kept
    total = mixed.shape[0]
    width = w_attn.shape[-1]
    heads = width // HEAD_DIM
    grad_final = live * grad_out
    grad_branch = grad_final.astype(jnp.bfloat16)
    grad_branch_all = gather_grads(grad_branch)
    g_bout = jnp.sum(grad_branch.astype(jnp.float32), axis=0)
    g_wout = inner(active, grad_branch_all)
    grad_active = by_transpose(grad_branch_all, w_out)
    unused, gelu_pull = jax.vjp(gelu_tanh, hidden)
    grad_hidden = gelu_pull(grad_active)[0].astype(jnp.bfloat16)
    g_bfc = jnp.sum(grad_hidden.astype(jnp.float32), axis=0)
    g_wfc = inner(normed_two_all, grad_hidden)
    grad_normed_two = grad_sum(grad_hidden, w_fc)
    unused, norm_pull = jax.vjp(layer_norm, middle, ln_gain[1], ln_bias[1])
    grad_middle, g_gain_two, g_shift_two = norm_pull(grad_normed_two)
    grad_middle = grad_middle + grad_final
    grad_attn = grad_middle.astype(jnp.bfloat16)
    grad_attn_all = gather_grads(grad_attn)
    g_bproj = jnp.sum(grad_attn.astype(jnp.float32), axis=0)
    g_wproj = inner(context, grad_attn_all)
    grad_context = (
        by_transpose(grad_attn_all, w_proj).astype(jnp.bfloat16).reshape(total, heads, HEAD_DIM)
    )
    queries = mixed[:, :width].reshape(total, heads, HEAD_DIM)
    keys = mixed[:, width : 2 * width].reshape(total, heads, HEAD_DIM)
    values = mixed[:, 2 * width :].reshape(total, heads, HEAD_DIM)
    grad_q, grad_k, grad_v = attend_backward(
        queries, keys, values, segment, logsum, grad_context, scale
    )
    grad_mixed = jnp.concatenate([grad_q, grad_k, grad_v], axis=1).astype(jnp.bfloat16)
    grad_wide = grad_mixed.astype(jnp.float32)
    g_bqv = jnp.stack(
        [jnp.sum(grad_wide[:, :width], axis=0), jnp.sum(grad_wide[:, 2 * width :], axis=0)]
    )
    g_wattn = inner(normed_all, grad_mixed).reshape(w_attn.shape)
    grad_normed = grad_sum(grad_mixed, w_attn.reshape(w_attn.shape[0], 3 * width))
    unused, first_pull = jax.vjp(layer_norm, rows, ln_gain[0], ln_bias[0])
    grad_rows, g_gain_one, g_shift_one = first_pull(grad_normed)
    grad_rows = grad_rows + grad_middle
    big = (g_wattn, g_wproj, g_wfc, g_wout)
    biases = (g_bqv, g_bfc)
    small = jnp.stack([g_gain_one, g_gain_two, g_shift_one, g_shift_two, g_bproj, g_bout])
    return (grad_rows, big, biases, small)


def add_tree(total, extra):
    if total is None:
        return extra
    return jax.tree.map(lambda left, right: left + right, total, extra)


def body(
    inputs,
    cotangent,
    seq_lengths,
    w_attn,
    b_qv,
    w_proj,
    b_proj,
    w_fc,
    b_fc,
    w_out,
    b_out,
    ln_gain,
    ln_bias,
):
    single = jnp.float32
    params = (
        w_attn[0],
        b_qv[0].astype(single),
        w_proj[0],
        b_proj[0].astype(single),
        w_fc[0],
        b_fc[0].astype(single),
        w_out[0],
        b_out[0].astype(single),
        ln_gain[0].astype(single),
        ln_bias[0].astype(single),
    )
    micro, own, width_model = inputs.shape
    total = own * lax.axis_size("tensor")
    own_start = lax.axis_index("tensor") * own
    first = lax.axis_index("section") == 0
    scale = HEAD_DIM ** (-0.5)
    masks = [masks_for(seq_lengths[0, index], total, own_start, own) for index in range(micro)]
    received = jnp.zeros((own, width_model), jnp.bfloat16)
    outputs = []
    kept_all = []
    for step in range(micro + 1):
        batch_first = min(step, micro - 1)
        batch_second = max(step - 1, 0)
        segment = jnp.where(first, masks[batch_first][0], masks[batch_second][0])
        live = jnp.where(first, masks[batch_first][1], masks[batch_second][1])
        rows = jnp.where(first, inputs[batch_first], received).astype(single)
        result, kept = forward_block(params, rows, segment, live, scale)
        outputs.append(result)
        kept_all.append((kept, segment, live))
        if step < micro:
            received = shifted(result, "section", 1)
    section_out = jnp.stack(
        [jnp.where(first, outputs[index], outputs[index + 1]) for index in range(micro)]
    )
    coming = jnp.zeros((own, width_model), single)
    sent_all = []
    big_total = None
    bias_total = None
    small_total = None
    for step in range(micro + 1):
        kept, segment, live = kept_all[micro - step]
        batch = micro - 1 - step
        if batch >= 0:
            from_end = cotangent[batch].astype(single)
        else:
            from_end = jnp.zeros((own, width_model), single)
        grad_out = jnp.where(first, coming, from_end)
        grad_rows, big, biases, small = backward_block(params, kept, grad_out, segment, live, scale)
        sent = grad_rows.astype(jnp.bfloat16)
        sent_all.append(sent)
        if step < micro:
            coming = shifted(sent, "section", -1).astype(single)
        big = (
            lax.psum_scatter(
                big[0].astype(jnp.bfloat16), "dp", scatter_dimension=0, tiled=True
            ).astype(jnp.float32),
            lax.psum_scatter(
                big[1].astype(jnp.bfloat16), "dp", scatter_dimension=1, tiled=True
            ).astype(jnp.float32),
            lax.psum_scatter(
                big[2].astype(jnp.bfloat16), "dp", scatter_dimension=0, tiled=True
            ).astype(jnp.float32),
            lax.psum_scatter(
                big[3].astype(jnp.bfloat16), "dp", scatter_dimension=1, tiled=True
            ).astype(jnp.float32),
        )
        big_total = add_tree(big_total, big)
        bias_total = add_tree(bias_total, biases)
        small_total = small if small_total is None else small_total + small
    g_bqv, g_bfc = lax.psum(bias_total, "dp")
    small_sum = lax.psum_scatter(small_total, ("dp", "tensor"), scatter_dimension=1, tiled=True)
    input_grad = jnp.stack(
        [
            jnp.where(first, sent_all[micro - index], sent_all[micro - 1 - index])
            for index in range(micro)
        ]
    )
    g_wattn, g_wproj, g_wfc, g_wout = big_total
    return (
        section_out[None],
        input_grad[None],
        g_wattn[None],
        g_bqv[None],
        g_wproj[None],
        small_sum[4][None],
        g_wfc[None],
        g_bfc[None],
        g_wout[None],
        small_sum[5][None],
        small_sum[0:2][None],
        small_sum[2:4][None],
    )


def solution(mesh):
    in_specs = (
        P(None, ("dp", "tensor"), None),
        P(None, ("dp", "tensor"), None),
        P("dp", None, None),
        P("section", None, None, "tensor"),
        P("section", None, "tensor"),
        P("section", "tensor", None),
        P("section", None),
        P("section", None, "tensor"),
        P("section", "tensor"),
        P("section", "tensor", None),
        P("section", None),
        P("section", None, None),
        P("section", None, None),
    )
    out_specs = (
        P("section", None, ("dp", "tensor"), None),
        P("section", None, ("dp", "tensor"), None),
        P("section", "dp", None, "tensor"),
        P("section", None, "tensor"),
        P("section", "tensor", "dp"),
        P("section", ("dp", "tensor")),
        P("section", "dp", "tensor"),
        P("section", "tensor"),
        P("section", "tensor", "dp"),
        P("section", ("dp", "tensor")),
        P("section", None, ("dp", "tensor")),
        P("section", None, ("dp", "tensor")),
    )
    return jax.shard_map(body, mesh=mesh, in_specs=in_specs, out_specs=out_specs, check_vma=False)
```

profile of v0, /device:TPU:0, one launch (start us, length us, event | category | flops | bytes accessed | tf_op | source)
XLA Modules:
  0.0 1544.2 jit_solution(17500441532649837994)
XLA Ops:
  30.6 23.6 %reduce-scatter.54.cloned.1.call-done = bf16[128,768]{1,0:T(8,128)(2,1)} async-done(((bf16[512,768]{1,0:T(8,128)(2,1)}), bf16[128,768]{1,0:T(8,128)(2,1)}) %reduce-scatter.54.cloned.1.call-update) | async-done | bytes 196624 | tf_op jit(solution)/shard_map/reduce_scatter | solution.py:56
  117.5 25.3 %reduce-scatter.58.cloned.1.call-done = bf16[128,768]{1,0:T(8,128)(2,1)} async-done(((bf16[512,768]{1,0:T(8,128)(2,1)}), bf16[128,768]{1,0:T(8,128)(2,1)}) %reduce-scatter.58.cloned.1.call-update) | async-done | bytes 196624 | tf_op jit(solution)/shard_map/reduce_scatter | solution.py:56
  164.0 19.9 %reduce-scatter.60.cloned.1.call-done = bf16[128,768]{1,0:T(8,128)(2,1)} async-done(((bf16[512,768]{1,0:T(8,128)(2,1)}), bf16[128,768]{1,0:T(8,128)(2,1)}) %reduce-scatter.60.cloned.1.call-update) | async-done | bytes 196624 | tf_op jit(solution)/shard_map/reduce_scatter | solution.py:56
  207.1 25.3 %reduce-scatter.62.cloned.1.call-done = bf16[128,768]{1,0:T(8,128)(2,1)} async-done(((bf16[512,768]{1,0:T(8,128)(2,1)}), bf16[128,768]{1,0:T(8,128)(2,1)}) %reduce-scatter.62.cloned.1.call-update) | async-done | bytes 196624 | tf_op jit(solution)/shard_map/reduce_scatter | solution.py:56
  249.7 23.7 %reduce-scatter.64.cloned.1.call-done = bf16[128,768]{1,0:T(8,128)(2,1)} async-done(((bf16[512,768]{1,0:T(8,128)(2,1)}), bf16[128,768]{1,0:T(8,128)(2,1)}) %reduce-scatter.64.cloned.1.call-update) | async-done | bytes 196624 | tf_op jit(solution)/shard_map/reduce_scatter | solution.py:56
  297.2 25.3 %reduce-scatter.66.cloned.1.call-done = bf16[128,768]{1,0:T(8,128)(2,1)} async-done(((bf16[512,768]{1,0:T(8,128)(2,1)}), bf16[128,768]{1,0:T(8,128)(2,1)}) %reduce-scatter.66.cloned.1.call-update) | async-done | bytes 196624 | tf_op jit(solution)/shard_map/reduce_scatter | solution.py:56
  340.5 23.8 %reduce-scatter.68.cloned.1.call-done = bf16[128,768]{1,0:T(8,128)(2,1)} async-done(((bf16[512,768]{1,0:T(8,128)(2,1)}), bf16[128,768]{1,0:T(8,128)(2,1)}) %reduce-scatter.68.cloned.1.call-update) | async-done | bytes 196624 | tf_op jit(solution)/shard_map/reduce_scatter | solution.py:56
  432.7 23.7 %reduce-scatter.74.cloned.1.call-done = bf16[128,768]{1,0:T(8,128)(2,1)} async-done(((bf16[512,768]{1,0:T(8,128)(2,1)}), bf16[128,768]{1,0:T(8,128)(2,1)}) %reduce-scatter.74.cloned.1.call-update) | async-done | bytes 196624 | tf_op jit(solution)/shard_map/reduce_scatter | solution.py:65
  478.0 23.8 %reduce-scatter.76.cloned.1.call-done = bf16[128,768]{1,0:T(8,128)(2,1)} async-done(((bf16[512,768]{1,0:T(8,128)(2,1)}), bf16[128,768]{1,0:T(8,128)(2,1)}) %reduce-scatter.76.cloned.1.call-update) | async-done | bytes 196624 | tf_op jit(solution)/shard_map/reduce_scatter | solution.py:65
  529.1 23.5 %reduce-scatter.78.cloned.1.call-done = bf16[128,768]{1,0:T(8,128)(2,1)} async-done(((bf16[512,768]{1,0:T(8,128)(2,1)}), bf16[128,768]{1,0:T(8,128)(2,1)}) %reduce-scatter.78.cloned.1.call-update) | async-done | bytes 196624 | tf_op jit(solution)/shard_map/reduce_scatter | solution.py:65
  574.8 23.6 %reduce-scatter.80.cloned.1.call-done = bf16[128,768]{1,0:T(8,128)(2,1)} async-done(((bf16[512,768]{1,0:T(8,128)(2,1)}), bf16[128,768]{1,0:T(8,128)(2,1)}) %reduce-scatter.80.cloned.1.call-update) | async-done | bytes 196624 | tf_op jit(solution)/shard_map/reduce_scatter | solution.py:65
  626.2 23.5 %reduce-scatter.82.cloned.1.call-done = bf16[128,768]{1,0:T(8,128)(2,1)} async-done(((bf16[512,768]{1,0:T(8,128)(2,1)}), bf16[128,768]{1,0:T(8,128)(2,1)}) %reduce-scatter.82.cloned.1.call-update) | async-done | bytes 196624 | tf_op jit(solution)/shard_map/reduce_scatter | solution.py:65
  671.4 23.8 %reduce-scatter.84.cloned.1.call-done = bf16[128,768]{1,0:T(8,128)(2,1)} async-done(((bf16[512,768]{1,0:T(8,128)(2,1)}), bf16[128,768]{1,0:T(8,128)(2,1)}) %reduce-scatter.84.cloned.1.call-update) | async-done | bytes 196624 | tf_op jit(solution)/shard_map/reduce_scatter | solution.py:65
  723.1 23.3 %reduce-scatter.86.cloned.1.call-done = bf16[128,768]{1,0:T(8,128)(2,1)} async-done(((bf16[512,768]{1,0:T(8,128)(2,1)}), bf16[128,768]{1,0:T(8,128)(2,1)}) %reduce-scatter.86.cloned.1.call-update) | async-done | bytes 196624 | tf_op jit(solution)/shard_map/reduce_scatter | solution.py:65
  768.6 23.8 %reduce-scatter.88.cloned.1.call-done = bf16[128,768]{1,0:T(8,128)(2,1)} async-done(((bf16[512,768]{1,0:T(8,128)(2,1)}), bf16[128,768]{1,0:T(8,128)(2,1)}) %reduce-scatter.88.cloned.1.call-update) | async-done | bytes 196624 | tf_op jit(solution)/shard_map/reduce_scatter | solution.py:65
  819.0 23.5 %reduce-scatter.90.cloned.1.call-done = bf16[128,768]{1,0:T(8,128)(2,1)} async-done(((bf16[512,768]{1,0:T(8,128)(2,1)}), bf16[128,768]{1,0:T(8,128)(2,1)}) %reduce-scatter.90.cloned.1.call-update) | async-done | bytes 196624 | tf_op jit(solution)/shard_map/reduce_scatter | solution.py:65
  1024.9 27.9 %reduce-scatter.114.cloned.1.call-done = bf16[768,192]{0,1:T(8,128)(2,1)} async-done(((bf16[768,768]{0,1:T(8,128)(2,1)}), bf16[768,192]{0,1:T(8,128)(2,1)}) %reduce-scatter.114.cloned.1.call-update) | async-done | bytes 294928 | tf_op jit(solution)/shard_map/reduce_scatter | solution.py:298
  1052.8 30.2 %reduce-scatter.116.cloned.1.call-done = bf16[768,192]{0,1:T(8,128)(2,1)} async-done(((bf16[768,768]{0,1:T(8,128)(2,1)}), bf16[768,192]{0,1:T(8,128)(2,1)}) %reduce-scatter.116.cloned.1.call-update) | async-done | bytes 294928 | tf_op jit(solution)/shard_map/reduce_scatter | solution.py:298
  1083.0 30.3 %reduce-scatter.118.cloned.1.call-done = bf16[768,192]{0,1:T(8,128)(2,1)} async-done(((bf16[768,768]{0,1:T(8,128)(2,1)}), bf16[768,192]{0,1:T(8,128)(2,1)}) %reduce-scatter.118.cloned.1.call-update) | async-done | bytes 294928 | tf_op jit(solution)/shard_map/reduce_scatter | solution.py:298
  1113.3 30.3 %reduce-scatter.120.cloned.1.call-done = bf16[768,192]{0,1:T(8,128)(2,1)} async-done(((bf16[768,768]{0,1:T(8,128)(2,1)}), bf16[768,192]{0,1:T(8,128)(2,1)}) %reduce-scatter.120.cloned.1.call-update) | async-done | bytes 294928 | tf_op jit(solution)/shard_map/reduce_scatter | solution.py:298
  1143.7 30.2 %reduce-scatter.122.cloned.1.call-done = bf16[768,192]{0,1:T(8,128)(2,1)} async-done(((bf16[768,768]{0,1:T(8,128)(2,1)}), bf16[768,192]{0,1:T(8,128)(2,1)}) %reduce-scatter.122.cloned.1.call-update) | async-done | bytes 294928 | tf_op jit(solution)/shard_map/reduce_scatter | solution.py:298
  1176.2 28.0 %reduce-scatter.104.cloned.1.call-done = bf16[192,768]{1,0:T(8,128)(2,1)} async-done(((bf16[768,768]{1,0:T(8,128)(2,1)}), bf16[192,768]{1,0:T(8,128)(2,1)}) %reduce-scatter.104.cloned.1.call-update) | async-done | bytes 294928 | tf_op jit(solution)/shard_map/reduce_scatter | solution.py:295
  1204.2 30.4 %reduce-scatter.106.cloned.1.call-done = bf16[192,768]{1,0:T(8,128)(2,1)} async-done(((bf16[768,768]{1,0:T(8,128)(2,1)}), bf16[192,768]{1,0:T(8,128)(2,1)}) %reduce-scatter.106.cloned.1.call-update) | async-done | bytes 294928 | tf_op jit(solution)/shard_map/reduce_scatter | solution.py:295
  1234.6 30.2 %reduce-scatter.108.cloned.1.call-done = bf16[192,768]{1,0:T(8,128)(2,1)} async-done(((bf16[768,768]{1,0:T(8,128)(2,1)}), bf16[192,768]{1,0:T(8,128)(2,1)}) %reduce-scatter.108.cloned.1.call-update) | async-done | bytes 294928 | tf_op jit(solution)/shard_map/reduce_scatter | solution.py:295
  1264.8 30.4 %reduce-scatter.110.cloned.1.call-done = bf16[192,768]{1,0:T(8,128)(2,1)} async-done(((bf16[768,768]{1,0:T(8,128)(2,1)}), bf16[192,768]{1,0:T(8,128)(2,1)}) %reduce-scatter.110.cloned.1.call-update) | async-done | bytes 294928 | tf_op jit(solution)/shard_map/reduce_scatter | solution.py:295
  1295.1 30.3 %reduce-scatter.112.cloned.1.call-done = bf16[192,768]{1,0:T(8,128)(2,1)} async-done(((bf16[768,768]{1,0:T(8,128)(2,1)}), bf16[192,768]{1,0:T(8,128)(2,1)}) %reduce-scatter.112.cloned.1.call-update) | async-done | bytes 294928 | tf_op jit(solution)/shard_map/reduce_scatter | solution.py:295
  1329.3 54.2 %reduce-scatter.134.cloned.1.call-done = f32[48,6]{1,0:T(8,128)} async-done(((f32[768,6]{1,0:T(8,128)}), f32[48,6]{1,0:T(8,128)}) %reduce-scatter.134.cloned.1.call-update) | async-done | bytes 1168
  1387.8 26.2 %reduce-scatter.94.cloned.1.call-done = bf16[192,3,192]{2,0,1:T(8,128)(2,1)} async-done(((bf16[768,3,192]{2,0,1:T(8,128)(2,1)}), bf16[192,3,192]{2,0,1:T(8,128)(2,1)}) %reduce-scatter.94.cloned.1.call-update) | async-done | bytes 221200 | tf_op jit(solution)/shard_map/reduce_scatter | solution.py:289
  1414.0 30.2 %reduce-scatter.96.cloned.1.call-done = bf16[192,3,192]{2,0,1:T(8,128)(2,1)} async-done(((bf16[768,3,192]{2,0,1:T(8,128)(2,1)}), bf16[192,3,192]{2,0,1:T(8,128)(2,1)}) %reduce-scatter.96.cloned.1.call-update) | async-done | bytes 221200 | tf_op jit(solution)/shard_map/reduce_scatter | solution.py:289
  1444.2 30.1 %reduce-scatter.98.cloned.1.call-done = bf16[192,3,192]{2,0,1:T(8,128)(2,1)} async-done(((bf16[768,3,192]{2,0,1:T(8,128)(2,1)}), bf16[192,3,192]{2,0,1:T(8,128)(2,1)}) %reduce-scatter.98.cloned.1.call-update) | async-done | bytes 221200 | tf_op jit(solution)/shard_map/reduce_scatter | solution.py:289
  1474.3 30.2 %reduce-scatter.100.cloned.1.call-done = bf16[192,3,192]{2,0,1:T(8,128)(2,1)} async-done(((bf16[768,3,192]{2,0,1:T(8,128)(2,1)}), bf16[192,3,192]{2,0,1:T(8,128)(2,1)}) %reduce-scatter.100.cloned.1.call-update) | async-done | bytes 221200 | tf_op jit(solution)/shard_map/reduce_scatter | solution.py:289
  1504.6 30.2 %reduce-scatter.102.cloned.1.call-done = bf16[192,3,192]{2,0,1:T(8,128)(2,1)} async-done(((bf16[768,3,192]{2,0,1:T(8,128)(2,1)}), bf16[192,3,192]{2,0,1:T(8,128)(2,1)}) %reduce-scatter.102.cloned.1.call-update) | async-done | bytes 221200 | tf_op jit(solution)/shard_map/reduce_scatter | solution.py:289
  (988 shorter events, 647.1 us)
Async XLA Ops:
  71.3 71.5 %reduce-scatter.58.cloned.1.call-start = ((), (), s32[]{:S(2)}) async-start(), calls=%async_computation.43 | async-start | bytes 983040 | tf_op jit(solution)/shard_map/reduce_scatter | solution.py:56
  160.2 72.3 %reduce-scatter.62.cloned.1.call-start = ((), (), s32[]{:S(2)}) async-start(), calls=%async_computation.45 | async-start | bytes 983040 | tf_op jit(solution)/shard_map/reduce_scatter | solution.py:56
  249.6 72.9 %reduce-scatter.66.cloned.1.call-start = ((), (), s32[]{:S(2)}) async-start(), calls=%async_computation.47 | async-start | bytes 983040 | tf_op jit(solution)/shard_map/reduce_scatter | solution.py:56
  340.4 72.9 %reduce-scatter.70.cloned.1.call-start = ((), (), s32[]{:S(2)}) async-start(), calls=%async_computation.49 | async-start | bytes 983040 | tf_op jit(solution)/shard_map/reduce_scatter | solution.py:56
  478.0 74.6 %reduce-scatter.78.cloned.1.call-start = ((), (), s32[]{:S(2)}) async-start(), calls=%async_computation.53 | async-start | bytes 983040 | tf_op jit(solution)/shard_map/reduce_scatter | solution.py:65
  529.1 69.3 %reduce-scatter.80.cloned.1.call-start = ((), (), s32[]{:S(2)}) async-start(), calls=%async_computation.54 | async-start | bytes 983040 | tf_op jit(solution)/shard_map/reduce_scatter | solution.py:65
  574.6 75.1 %reduce-scatter.82.cloned.1.call-start = ((), (), s32[]{:S(2)}) async-start(), calls=%async_computation.55 | async-start | bytes 983040 | tf_op jit(solution)/shard_map/reduce_scatter | solution.py:65
  671.3 75.1 %reduce-scatter.86.cloned.1.call-start = ((), (), s32[]{:S(2)}) async-start(), calls=%async_computation.57 | async-start | bytes 983040 | tf_op jit(solution)/shard_map/reduce_scatter | solution.py:65
  722.9 69.5 %reduce-scatter.88.cloned.1.call-start = ((), (), s32[]{:S(2)}) async-start(), calls=%async_computation.58 | async-start | bytes 983040 | tf_op jit(solution)/shard_map/reduce_scatter | solution.py:65
  768.5 73.9 %reduce-scatter.90.cloned.1.call-start = ((), (), s32[]{:S(2)}) async-start(), calls=%async_computation.59 | async-start | bytes 983040 | tf_op jit(solution)/shard_map/reduce_scatter | solution.py:65
  818.9 95.3 %reduce-scatter.92.cloned.1.call-start = ((), (), s32[]{:S(2)}) async-start(), calls=%async_computation.60 | async-start | bytes 983040 | tf_op jit(solution)/shard_map/reduce_scatter | solution.py:65
  866.7 74.9 %reduce-scatter.124.cloned.1.call-start = ((), (), s32[]{:S(2)}) async-start(), calls=%async_computation.76 | async-start | bytes 491520
  869.0 88.7 %reduce-scatter.126.cloned.1.call-start = ((), (), s32[]{:S(2)}) async-start(), calls=%async_computation.77 | async-start | bytes 491520
  871.5 107.8 %reduce-scatter.128.cloned.1.call-start = ((), (), s32[]{:S(2)}) async-start(), calls=%async_computation.78 | async-start | bytes 491520
  873.8 127.3 %reduce-scatter.130.cloned.1.call-start = ((), (), s32[]{:S(2)}) async-start(), calls=%async_computation.79 | async-start | bytes 491520
  876.4 146.6 %reduce-scatter.132.cloned.1.call-start = ((), (), s32[]{:S(2)}) async-start(), calls=%async_computation.80 | async-start | bytes 491520
  878.7 174.1 %reduce-scatter.114.cloned.1.call-start = ((), (), s32[]{:S(2)}) async-start(), calls=%async_computation.71 | async-start | bytes 1474560 | tf_op jit(solution)/shard_map/reduce_scatter | solution.py:298
  882.6 200.4 %reduce-scatter.116.cloned.1.call-start = ((), (), s32[]{:S(2)}) async-start(), calls=%async_computation.72 | async-start | bytes 1474560 | tf_op jit(solution)/shard_map/reduce_scatter | solution.py:298
  886.2 227.2 %reduce-scatter.118.cloned.1.call-start = ((), (), s32[]{:S(2)}) async-start(), calls=%async_computation.73 | async-start | bytes 1474560 | tf_op jit(solution)/shard_map/reduce_scatter | solution.py:298
  890.0 253.7 %reduce-scatter.120.cloned.1.call-start = ((), (), s32[]{:S(2)}) async-start(), calls=%async_computation.74 | async-start | bytes 1474560 | tf_op jit(solution)/shard_map/reduce_scatter | solution.py:298
  893.5 280.4 %reduce-scatter.122.cloned.1.call-start = ((), (), s32[]{:S(2)}) async-start(), calls=%async_computation.75 | async-start | bytes 1474560 | tf_op jit(solution)/shard_map/reduce_scatter | solution.py:298
  897.4 306.8 %reduce-scatter.104.cloned.1.call-start = ((), (), s32[]{:S(2)}) async-start(), calls=%async_computation.66 | async-start | bytes 1474560 | tf_op jit(solution)/shard_map/reduce_scatter | solution.py:295
  900.5 334.0 %reduce-scatter.106.cloned.1.call-start = ((), (), s32[]{:S(2)}) async-start(), calls=%async_computation.67 | async-start | bytes 1474560 | tf_op jit(solution)/shard_map/reduce_scatter | solution.py:295
  903.9 360.9 %reduce-scatter.108.cloned.1.call-start = ((), (), s32[]{:S(2)}) async-start(), calls=%async_computation.68 | async-start | bytes 1474560 | tf_op jit(solution)/shard_map/reduce_scatter | solution.py:295
  907.0 388.1 %reduce-scatter.110.cloned.1.call-start = ((), (), s32[]{:S(2)}) async-start(), calls=%async_computation.69 | async-start | bytes 1474560 | tf_op jit(solution)/shard_map/reduce_scatter | solution.py:295
  910.4 415.1 %reduce-scatter.112.cloned.1.call-start = ((), (), s32[]{:S(2)}) async-start(), calls=%async_computation.70 | async-start | bytes 1474560 | tf_op jit(solution)/shard_map/reduce_scatter | solution.py:295
  913.5 470.0 %reduce-scatter.134.cloned.1.call-start = ((), (), s32[]{:S(2)}) async-start(), calls=%async_computation.81 | async-start | bytes 417792
  918.3 495.8 %reduce-scatter.94.cloned.1.call-start = ((), (), s32[]{:S(2)}) async-start(), calls=%async_computation.61 | async-start | bytes 1474560 | tf_op jit(solution)/shard_map/reduce_scatter | solution.py:289
  921.8 522.5 %reduce-scatter.96.cloned.1.call-start = ((), (), s32[]{:S(2)}) async-start(), calls=%async_computation.62 | async-start | bytes 1474560 | tf_op jit(solution)/shard_map/reduce_scatter | solution.py:289
  925.3 549.0 %reduce-scatter.98.cloned.1.call-start = ((), (), s32[]{:S(2)}) async-start(), calls=%async_computation.63 | async-start | bytes 1474560 | tf_op jit(solution)/shard_map/reduce_scatter | solution.py:289
  928.9 575.6 %reduce-scatter.100.cloned.1.call-start = ((), (), s32[]{:S(2)}) async-start(), calls=%async_computation.64 | async-start | bytes 1474560 | tf_op jit(solution)/shard_map/reduce_scatter | solution.py:289
  938.4 596.4 %reduce-scatter.102.cloned.1.call-start = ((), (), s32[]{:S(2)}) async-start(), calls=%async_computation.65 | async-start | bytes 1474560 | tf_op jit(solution)/shard_map/reduce_scatter | solution.py:289
  (283 other events, 7103.8 us)
Sparse Core Ops, SparseCore 0:
  30.0 24.1 reduce-scatter.53
  71.4 23.6 reduce-scatter.55
  117.6 25.1 reduce-scatter.57
  160.3 23.6 reduce-scatter.59
  207.2 25.1 reduce-scatter.61
  249.7 23.6 reduce-scatter.63
  297.3 25.1 reduce-scatter.65
  340.5 23.6 reduce-scatter.67
  388.0 25.1 reduce-scatter.69
  432.8 23.6 reduce-scatter.73
  478.1 23.6 reduce-scatter.75
  574.7 23.6 reduce-scatter.79
  626.2 23.3 reduce-scatter.81
  671.4 23.6 reduce-scatter.83
  768.7 23.6 reduce-scatter.87
  863.3 23.6 reduce-scatter.91
  1025.3 27.4 reduce-scatter.113
  1055.1 27.8 reduce-scatter.115
  1085.4 27.8 reduce-scatter.117
  1115.8 27.8 reduce-scatter.119
  1145.9 27.8 reduce-scatter.121
  1176.3 27.8 reduce-scatter.103
  1206.6 27.8 reduce-scatter.105
  1236.8 27.9 reduce-scatter.107
  1267.2 27.8 reduce-scatter.109
  1297.6 27.8 reduce-scatter.111
  1329.2 54.2 reduce-scatter.133
  1385.7 28.2 reduce-scatter.93
  1416.3 27.8 reduce-scatter.95
  1446.4 27.8 reduce-scatter.97
  1476.6 27.8 reduce-scatter.99
  1506.9 27.8 reduce-scatter.101
  (9 shorter events, 189.1 us)
where the time goes:
time: 1550 us; the launch traced here: 1540 us
  waiting for transfers between devices  1010 us (65%)
  blocking collectives  173 us (11%)
  matrix products  128 us (8%)
  other arithmetic  123 us (8%)
  local copies, waits for them, and re-layouts  66.4 us (4%)
  starting transfers between devices  21.1 us (1%)
  between operations  18.2 us (1%)
    reduce_scatter x10, waiting for transfers between devices, grad_sum(): lax.psum_scatter(by_transpose(left, weight).astype(jnp.bfloat16), 'tensor...  212 us
    reduce_scatter x10, waiting for transfers between devices, row_sum(): lax.psum_scatter(jnp.dot(left, weight, preferred_element_type=jnp.float32...  202 us
    reduce_scatter x5, waiting for transfers between devices, body(): lax.psum_scatter(big[2].astype(jnp.bfloat16), 'dp', scatter_dimension=0,...  149 us
    reduce_scatter x5, waiting for transfers between devices, body(): lax.psum_scatter(big[3].astype(jnp.bfloat16), 'dp', scatter_dimension=1,...  149 us
    reduce_scatter x5, waiting for transfers between devices, body(): lax.psum_scatter(big[0].astype(jnp.bfloat16), 'dp', scatter_dimension=0,...  147 us
    unnamed x47, waiting for transfers between devices  111 us
    all_gather x10, blocking collectives, gather_rows(): return lax.all_gather(normed, 'tensor', axis=0, tiled=True)  82.1 us
    all_gather x10, blocking collectives, gather_grads(): return lax.all_gather(grads, 'tensor', axis=0, tiled=True)  81.1 us
  transfers between devices with their start and end apart: 49, of which 46 were waited for; matrix products, arithmetic and copies ran while one was open for 7% of the time, Pallas kernels for 0%

commit v1 on v0

v1 whole, which is shorter than its diff:
```python
import functools

import jax
import jax.numpy as jnp
from jax import lax
from jax.experimental import pallas as pl
from jax.experimental.pallas import tpu as pltpu
from jax.sharding import PartitionSpec as P

HEAD_DIM = 64
SCALE = HEAD_DIM**-0.5
F32 = jnp.float32
BF16 = jnp.bfloat16


def dot(left, right, dims):
    return lax.dot_general(left, right, (dims, ((), ())), preferred_element_type=F32)


NN = ((1,), (0,))
NT = ((1,), (1,))
TN = ((0,), (0,))


def layer_norm(rows, gain, shift):
    center = jnp.mean(rows, axis=-1, keepdims=True)
    centred = rows - center
    variance = jnp.mean(centred * centred, axis=-1, keepdims=True)
    return centred * lax.rsqrt(variance + 1e-05) * gain + shift


def gelu_tanh(values):
    return jax.nn.gelu(values, approximate=True)


def fill_mask(seg_col, seg_row, mask):
    total = mask.shape[0]
    query = lax.broadcasted_iota(jnp.int32, (total, total), 0)
    key = lax.broadcasted_iota(jnp.int32, (total, total), 1)
    allowed = (seg_col[...] == seg_row[...]) & (key <= query)
    mask[...] = jnp.where(allowed, 0.0, -1e30)


def bands(total):
    span = total // 2 if total % 256 == 0 else total
    return [(start, span, start + span) for start in range(0, total, span)]


def attend_kernel(heads, mixed, seg_col, seg_row, context, mask):
    fill_mask(seg_col, seg_row, mask)
    width = heads * HEAD_DIM
    total = mixed.shape[0]
    every = mixed[...]
    parts = []
    for head in range(heads):
        at = head * HEAD_DIM
        queries = every[:, at : at + HEAD_DIM] * SCALE
        keys = every[:, width + at : width + at + HEAD_DIM]
        values = every[:, 2 * width + at : 2 * width + at + HEAD_DIM]
        rows = []
        for start, span, seen in bands(total):
            scores = dot(queries[start : start + span], keys[:seen], NT)
            scores = scores + mask[start : start + span, :seen]
            expo = jnp.exp(scores - jnp.max(scores, axis=-1, keepdims=True))
            weights = expo / jnp.sum(expo, axis=-1, keepdims=True)
            rows.append(dot(weights.astype(BF16), values[:seen], NN))
        parts.append(jnp.concatenate(rows, axis=0))
    context[...] = jnp.concatenate(parts, axis=1).astype(BF16)


def attend_grad_kernel(heads, mixed, grad_context, seg_col, seg_row, grad_mixed, mask):
    fill_mask(seg_col, seg_row, mask)
    width = heads * HEAD_DIM
    total = mixed.shape[0]
    every = mixed[...]
    grads = grad_context[...]
    all_q, all_k, all_v = [], [], []
    for head in range(heads):
        at = head * HEAD_DIM
        queries = every[:, at : at + HEAD_DIM] * SCALE
        keys = every[:, width + at : width + at + HEAD_DIM]
        values = every[:, 2 * width + at : 2 * width + at + HEAD_DIM]
        grad = grads[:, at : at + HEAD_DIM]
        grad_q, grad_k, grad_v = [], [], []
        for start, span, seen in bands(total):
            here = queries[start : start + span]
            grad_here = grad[start : start + span]
            scores = dot(here, keys[:seen], NT) + mask[start : start + span, :seen]
            expo = jnp.exp(scores - jnp.max(scores, axis=-1, keepdims=True))
            probs = expo / jnp.sum(expo, axis=-1, keepdims=True)
            grad_v.append(dot(probs.astype(BF16), grad_here, TN))
            grad_probs = dot(grad_here, values[:seen], NT)
            weighted = jnp.sum(probs * grad_probs, axis=-1, keepdims=True)
            grad_scores = (probs * (grad_probs - weighted)).astype(BF16)
            grad_q.append(dot(grad_scores, keys[:seen], NN) * SCALE)
            grad_k.append(dot(grad_scores, here, TN))
        for pieces, whole in ((grad_k, all_k), (grad_v, all_v)):
            summed = pieces[-1]
            for piece in pieces[:-1]:
                rest = summed.shape[0] - piece.shape[0]
                summed = jnp.concatenate(
                    [summed[: piece.shape[0]] + piece, summed[piece.shape[0] :]], axis=0
                ) if rest else summed + piece
            whole.append(summed)
        all_q.append(jnp.concatenate(grad_q, axis=0))
    grad_mixed[...] = jnp.concatenate(all_q + all_k + all_v, axis=1).astype(BF16)


def attend(mixed, segment):
    total, width = mixed.shape
    width //= 3
    heads = width // HEAD_DIM
    return pl.pallas_call(
        functools.partial(attend_kernel, heads),
        out_shape=jax.ShapeDtypeStruct((total, width), BF16),
        scratch_shapes=[pltpu.VMEM((total, total), F32)],
        compiler_params=pltpu.CompilerParams(vmem_limit_bytes=32 * 2**20),
        cost_estimate=pl.CostEstimate(
            flops=3 * total * total * width, bytes_accessed=8 * total * width, transcendentals=heads * total * total
        ),
        name="attend",
    )(mixed, segment[:, None], segment[None, :])


def attend_grad(mixed, grad_context, segment):
    total, width = grad_context.shape
    heads = width // HEAD_DIM
    return pl.pallas_call(
        functools.partial(attend_grad_kernel, heads),
        out_shape=jax.ShapeDtypeStruct(mixed.shape, BF16),
        scratch_shapes=[pltpu.VMEM((total, total), F32)],
        compiler_params=pltpu.CompilerParams(vmem_limit_bytes=32 * 2**20),
        cost_estimate=pl.CostEstimate(
            flops=8 * total * total * width, bytes_accessed=14 * total * width, transcendentals=heads * total * total
        ),
        name="attend_grad",
    )(mixed, grad_context, segment[:, None], segment[None, :])


def partner(values, distance):
    return lax.ppermute(values, "tensor", [(i, i ^ distance) for i in range(4)])


def gather_four(own):
    far = partner(own, 2)
    return [own, partner(own, 1), far, partner(far, 1)]


def straight(pieces, index):
    odd = (index & 1) == 1
    upper = (index & 2) == 2
    low = [jnp.where(odd, pieces[k ^ 1], pieces[k]) for k in range(4)]
    return [jnp.where(upper, low[k ^ 2], low[k]) for k in range(4)]


def rows_to_batches(blocks, index):
    pieces = [lax.dynamic_index_in_dim(blocks, index ^ k, 0, keepdims=False) for k in range(4)]
    pieces = [pieces[0]] + [partner(pieces[k], k) for k in range(1, 4)]
    return jnp.concatenate(straight(pieces, index), axis=0)


def batches_to_rows(rows, index):
    own = rows.shape[0] // 4
    pieces = [lax.dynamic_slice_in_dim(rows, (index ^ k) * own, own, 0) for k in range(4)]
    pieces = [pieces[0]] + [partner(pieces[k], k) for k in range(1, 4)]
    return jnp.stack(straight(pieces, index))


def scatter_dp(values):
    count = lax.axis_size("dp")
    if count > 8:
        return lax.psum_scatter(values.astype(BF16), "dp", scatter_dimension=0, tiled=True).astype(F32)
    share = values.shape[0] // count
    me = lax.axis_index("dp")
    total = lax.dynamic_slice_in_dim(values, me * share, share, 0)
    values = values.astype(BF16)
    for step in range(1, count):
        piece = lax.dynamic_slice_in_dim(values, lax.rem(me + step, count) * share, share, 0)
        route = [(i, (i + step) % count) for i in range(count)]
        total = total + lax.ppermute(piece, "dp", route).astype(F32)
    return total


def reduce_unit(grads):
    near = partner(grads[1].astype(BF16), 1)
    cross = partner(grads[3].astype(BF16), 1)
    send = (grads[2] + cross.astype(F32)).astype(BF16)
    own = grads[0] + near.astype(F32)
    return scatter_dp(own + partner(send, 2).astype(F32))


def forward(params, rows, segment, live):
    units, biases, b_proj, b_out, ln_gain, ln_bias = params
    attn, fc, out = units
    b_q, b_v, b_fc = biases
    width = b_q[0].shape[0]
    normed = layer_norm(rows, ln_gain[0], ln_bias[0]).astype(BF16)
    middle = rows + b_proj
    mixed_all, context_all = [], []
    for k in range(4):
        bias_row = jnp.concatenate([b_q[k], jnp.zeros_like(b_q[k]), b_v[k]])
        mixed = (dot(normed, attn[k][:, : 3 * width], NN) + bias_row).astype(BF16)
        context = attend(mixed, segment)
        middle = middle + dot(context, attn[k][:, 3 * width :], NT)
        mixed_all.append(mixed)
        context_all.append(context)
    normed_two = layer_norm(middle, ln_gain[1], ln_bias[1]).astype(BF16)
    result = middle + b_out
    hidden_all, active_all = [], []
    for k in range(4):
        hidden = dot(normed_two, fc[k], NN) + b_fc[k]
        active = gelu_tanh(hidden).astype(BF16)
        result = result + dot(active, out[k], NN)
        hidden_all.append(hidden)
        active_all.append(active)
    result = (live * result).astype(BF16)
    return result, (rows, normed, mixed_all, context_all, middle, normed_two, hidden_all, active_all)


def backward(params, kept, grad_out, segment, live, with_weights):
    units, biases, b_proj, b_out, ln_gain, ln_bias = params
    attn, fc, out = units
    rows, normed, mixed_all, context_all, middle, normed_two, hidden_all, active_all = kept
    width = biases[0][0].shape[0]
    grad_final = live * grad_out
    grad_branch = grad_final.astype(BF16)
    grad_normed_two = None
    grad_hidden_all, big_out, big_fc, big_attn = [], [], [], []
    for k in range(4):
        grad_active = dot(grad_branch, out[k], NT)
        unused, gelu_pull = jax.vjp(gelu_tanh, hidden_all[k])
        grad_hidden = gelu_pull(grad_active)[0].astype(BF16)
        part = dot(grad_hidden, fc[k], NT)
        grad_normed_two = part if k == 0 else grad_normed_two + part
        grad_hidden_all.append(grad_hidden)
    if with_weights:
        big_out = [dot(grad_branch, active_all[k], TN) for k in range(4)]
        big_fc = [dot(normed_two, grad_hidden_all[k], TN) for k in range(4)]
    unused, norm_pull = jax.vjp(layer_norm, middle, ln_gain[1], ln_bias[1])
    grad_middle, g_gain_two, g_shift_two = norm_pull(grad_normed_two)
    grad_middle = grad_middle + grad_final
    grad_attn = grad_middle.astype(BF16)
    grad_normed = None
    grad_mixed_all = []
    for k in range(4):
        grad_context = dot(grad_attn, attn[k][:, 3 * width :], NN).astype(BF16)
        grad_mixed = attend_grad(mixed_all[k], grad_context, segment)
        part = dot(grad_mixed, attn[k][:, : 3 * width], NT)
        grad_normed = part if k == 0 else grad_normed + part
        grad_mixed_all.append(grad_mixed)
    unused, first_pull = jax.vjp(layer_norm, rows, ln_gain[0], ln_bias[0])
    grad_rows, g_gain_one, g_shift_one = first_pull(grad_normed)
    grad_rows = (grad_rows + grad_middle).astype(BF16)
    if not with_weights:
        return grad_rows
    big_attn = [
        jnp.concatenate(
            [dot(normed, grad_mixed_all[k], TN), dot(grad_attn, context_all[k], TN)], axis=1
        )
        for k in range(4)
    ]
    split = [
        jnp.concatenate(
            [
                jnp.sum(grad_mixed_all[k][:, :width].astype(F32), axis=0),
                jnp.sum(grad_mixed_all[k][:, 2 * width :].astype(F32), axis=0),
                jnp.sum(grad_hidden_all[k].astype(F32), axis=0),
            ]
        )
        for k in range(4)
    ]
    small = jnp.concatenate(
        [
            g_gain_one,
            g_gain_two,
            g_shift_one,
            g_shift_two,
            jnp.sum(grad_attn.astype(F32), axis=0),
            jnp.sum(grad_branch.astype(F32), axis=0),
        ]
    )
    return grad_rows, (big_attn, big_fc, big_out), split, small


def body(
    inputs,
    cotangent,
    seq_lengths,
    w_attn,
    b_qv,
    w_proj,
    b_proj,
    w_fc,
    b_fc,
    w_out,
    b_out,
    ln_gain,
    ln_bias,
):
    micro, own, model = inputs.shape
    total = own * lax.axis_size("tensor")
    width = w_attn.shape[-1]
    me = lax.axis_index("tensor")
    first = lax.axis_index("section") == 0

    unit_attn = jnp.concatenate([w_attn[0].reshape(model, 3 * width), w_proj[0].T], axis=1)
    units = (gather_four(unit_attn), gather_four(w_fc[0]), gather_four(w_out[0]))
    split_own = jnp.concatenate([b_qv[0, 0], b_qv[0, 1], b_fc[0]])
    split_all = [v.astype(F32) for v in gather_four(split_own)]
    biases = (
        [v[:width] for v in split_all],
        [v[width : 2 * width] for v in split_all],
        [v[2 * width :] for v in split_all],
    )
    params = (
        units,
        biases,
        b_proj[0].astype(F32),
        b_out[0].astype(F32),
        ln_gain[0].astype(F32),
        ln_bias[0].astype(F32),
    )

    lengths = lax.dynamic_index_in_dim(seq_lengths[0], me, 0, keepdims=False)
    ends = jnp.cumsum(lengths)
    position = jnp.arange(total, dtype=jnp.int32)
    segment = jnp.sum((position[:, None] >= ends[None, :]).astype(jnp.int32), axis=1)
    live = (position < ends[-1]).astype(F32)[:, None]

    staged = rows_to_batches(jnp.where(first, inputs, cotangent), me)
    result, unused = forward(params, staged.astype(F32), segment, live)
    received = lax.ppermute(result, "section", [(0, 1)])
    rows = jnp.where(first, staged, received).astype(F32)
    result, kept = forward(params, rows, segment, live)
    section_out = batches_to_rows(result, me)
    sent = backward(params, kept, staged.astype(F32), segment, live, False)
    coming = lax.ppermute(sent, "section", [(1, 0)])
    grad_out = jnp.where(first, coming, staged).astype(F32)
    grad_rows, big, split, small = backward(params, kept, grad_out, segment, live, True)
    input_grad = batches_to_rows(grad_rows, me)

    g_attn, g_fc, g_out = [reduce_unit(grads) for grads in big]
    g_wattn = g_attn[:, : 3 * width].reshape(-1, 3, width)
    g_wproj = g_attn[:, 3 * width :].T
    g_wout = g_out.T

    flat = lax.psum(jnp.concatenate(straight(split, me) + [small]), ("dp", "tensor"))
    piece = split[0].shape[0]
    mine = lax.dynamic_slice_in_dim(flat, me * piece, piece, 0)
    g_bqv = mine[: 2 * width].reshape(2, width)
    g_bfc = mine[2 * width :]
    sums = flat[4 * piece :].reshape(6, model)
    share = model // (lax.axis_size("dp") * lax.axis_size("tensor"))
    place = (lax.axis_index("dp") * lax.axis_size("tensor") + me) * share
    sums = lax.dynamic_slice_in_dim(sums, place, share, 1)
    return (
        section_out[None],
        input_grad[None],
        g_wattn[None],
        g_bqv[None],
        g_wproj[None],
        sums[4][None],
        g_fc[None],
        g_bfc[None],
        g_wout[None],
        sums[5][None],
        sums[0:2][None],
        sums[2:4][None],
    )


def solution(mesh):
    in_specs = (
        P(None, ("dp", "tensor"), None),
        P(None, ("dp", "tensor"), None),
        P("dp", None, None),
        P("section", None, None, "tensor"),
        P("section", None, "tensor"),
        P("section", "tensor", None),
        P("section", None),
        P("section", None, "tensor"),
        P("section", "tensor"),
        P("section", "tensor", None),
        P("section", None),
        P("section", None, None),
        P("section", None, None),
    )
    out_specs = (
        P("section", None, ("dp", "tensor"), None),
        P("section", None, ("dp", "tensor"), None),
        P("section", "dp", None, "tensor"),
        P("section", None, "tensor"),
        P("section", "tensor", "dp"),
        P("section", ("dp", "tensor")),
        P("section", "dp", "tensor"),
        P("section", "tensor"),
        P("section", "tensor", "dp"),
        P("section", ("dp", "tensor")),
        P("section", None, ("dp", "tensor")),
        P("section", None, ("dp", "tensor")),
    )
    return jax.shard_map(body, mesh=mesh, in_specs=in_specs, out_specs=out_specs, check_vma=False)
```

time: 1550 us -> 587 us (0.38)
  waiting for transfers between devices: 1010 us -> 195 us
  blocking collectives: 173 us -> 60 us
  other arithmetic: 123 us -> 35.7 us
  Pallas kernels: 0 us -> 59.5 us
  matrix products: 128 us -> 162 us
  local copies, waits for them, and re-layouts: 66.4 us -> 32.5 us
    reduce_scatter x35 -> x0, waiting for transfers between devices: 860 us -> none  [the longest x10 212 us: grad_sum(): lax.psum_scatter(by_transpose(left, weight).astype(jnp.bfloat16), 'tensor...]
    all_gather x20 -> x0, blocking collectives: 163 us -> none  [the longest x10 82.1 us: gather_rows(): return lax.all_gather(normed, 'tensor', axis=0, tiled=True)]
    ppermute x8 -> x41, waiting for transfers between devices: 44 us -> 195 us  [the longest x30 136 us: partner(): return lax.ppermute(values, 'tensor', [(i, i ^ distance) for i in range(4)])]
    unnamed x47 -> x0, waiting for transfers between devices: 111 us -> none
    pallas_call x0 -> x16, Pallas kernels: none -> 59.5 us  [the longest x8 37.5 us: attend_grad(): pl.pallas_call(functools.partial(attend_grad_kernel, heads), out_shape=ja...]
    psum x1, blocking collectives: 9.42 us -> 60 us  [body(): lax.psum(jnp.concatenate(straight(split, me) + [small]), ('dp', 'tensor'))]
    unnamed x547 -> x308, local copies, waits for them, and re-layouts: 51.3 us -> 14.2 us
    dot_general x90 -> x72, matrix products: 128 us -> 162 us  [dot(): lax.dot_general(left, right, (dims, ((), ())), preferred_element_type=F32)]
  transfers between devices with their start and end apart: 49 -> 41, of which waited for: 46 -> 15; matrix products, arithmetic and copies ran while one was open for 7% -> 23% of each run, Pallas kernels for 0% -> 5%
where the time goes in v1:
time: 587 us; the launch traced here: 577 us
  waiting for transfers between devices  195 us (33%)
  matrix products  162 us (28%)
  blocking collectives  60 us (10%)
  Pallas kernels  59.5 us (10%)
  other arithmetic  35.7 us (6%)
  local copies, waits for them, and re-layouts  32.5 us (6%)
  starting transfers between devices  29 us (5%)
    dot_general x72, matrix products, dot(): lax.dot_general(left, right, (dims, ((), ())), preferred_element_type=F32)  162 us
    ppermute x30, waiting for transfers between devices, partner(): return lax.ppermute(values, 'tensor', [(i, i ^ distance) for i in range(4)])  136 us
    psum x1, blocking collectives, body(): lax.psum(jnp.concatenate(straight(split, me) + [small]), ('dp', 'tensor'))  60 us
    pallas_call x8, Pallas kernels, attend_grad(): pl.pallas_call(functools.partial(attend_grad_kernel, heads), out_shape=ja...  37.5 us
    ppermute x9, waiting for transfers between devices, scatter_dp(): total = total + lax.ppermute(piece, 'dp', route).astype(F32)  31.7 us
    pallas_call x8, Pallas kernels, attend(): pl.pallas_call(functools.partial(attend_kernel, heads), out_shape=jax.Sha...  22.1 us
    ppermute x1, waiting for transfers between devices, body(): received = lax.ppermute(result, 'section', [(0, 1)])  17.4 us
    ppermute x30, starting transfers between devices, partner(): return lax.ppermute(values, 'tensor', [(i, i ^ distance) for i in range(4)])  14.7 us
  transfers between devices with their start and end apart: 41, of which 15 were waited for; matrix products, arithmetic and copies ran while one was open for 23% of the time, Pallas kernels for 5%

profile of v1, /device:TPU:0, one launch (start us, length us, event | category | flops | bytes accessed | tf_op | source)
XLA Modules:
  0.0 577.2 jit_solution(4576906397581865992)
XLA Ops:
  14.8 25.1 %collective-permute-done = bf16[128,768]{1,0:T(8,128)(2,1)S(1)} collective-permute-done((bf16[128,768]{1,0:T(8,128)(2,1)S(1)}, bf16[128,768]{1,0:T(8,128)(2,1)S(1)}, u32[]{:S(2)}, u32[]{:S(2)}) %collective-permute-start) | collective-permute-done | bytes 196640 | tf_op jit(solution)/shard_map/ppermute | solution.py:141
  40.4 4.6 collective-permute-done.1
  54.8 15.6 %collective-permute-done.12 = bf16[768,768]{1,0:T(8,128)(2,1)} collective-permute-done((bf16[768,768]{1,0:T(8,128)(2,1)}, bf16[768,768]{1,0:T(8,128)(2,1)}, u32[]{:S(2)}, u32[]{:S(2)}) %collective-permute-start.12) | collective-permute-done | bytes 1179680 | tf_op jit(solution)/shard_map/ppermute | solution.py:141
  70.9 24.4 %collective-permute-done.11 = bf16[768,768]{1,0:T(8,128)(2,1)} collective-permute-done((bf16[768,768]{1,0:T(8,128)(2,1)}, bf16[768,768]{1,0:T(8,128)(2,1)}, u32[]{:S(2)}, u32[]{:S(2)}) %collective-permute-start.11) | collective-permute-done | bytes 1179680 | tf_op jit(solution)/shard_map/ppermute | solution.py:141
  107.3 4.4 fusion.91
  111.6 4.4 fusion.89
  116.0 4.4 fusion.90
  120.4 5.6 multiply_convert_fusion.5
  129.8 17.4 %collective-permute-done.15 = bf16[512,768]{1,0:T(8,128)(2,1)S(1)} collective-permute-done((bf16[512,768]{1,0:T(8,128)(2,1)}, bf16[512,768]{1,0:T(8,128)(2,1)S(1)}, u32[]{:S(2)}, u32[]{:S(2)}) %collective-permute-start.15) | collective-permute-done | bytes 786464 | tf_op jit(solution)/shard_map/ppermute | solution.py:332
  172.7 5.4 fusion.115
  178.2 4.0 fusion.168
  191.9 5.4 fusion.117
  197.3 5.4 fusion.116
  202.7 7.7 %multiply_reduce_fusion.2 = (f32[512]{0:T(512)S(1)}, f32[512,768]{1,0:T(8,128)}) fusion(f32[512,768]{1,0:T(8,128)} %copy-done.21, f32[512]{0:T(512)S(1)} %broadcast_multiply_fusion, f32[768]{0:T(1024)S(1)} %get-tuple-element.75, bf16[768,768]{1,0:T(8,128)(2,1)} %collective-permute-done.13, f32[512,768]{1,0:T(8,128)} %convolution_add_fusion, ...), kind=kOutput, calls=%fused_computation.129 | convolution fusion | flops 1222508032 | bytes 12592128 | tf_op jit(solution)/shard_map/dot_general | solution.py:17
  218.4 4.6 attend_grad.11
  227.8 4.6 attend_grad.10
  236.0 4.8 attend_grad.8
  247.6 4.6 attend_grad.9
  270.6 10.0 %collective-permute-done.19 = bf16[512,768]{1,0:T(8,128)(2,1)S(1)} collective-permute-done((bf16[512,768]{1,0:T(8,128)(2,1)S(1)}, bf16[512,768]{1,0:T(8,128)(2,1)S(1)}, u32[]{:S(2)}, u32[]{:S(2)}) %collective-permute-start.19) | collective-permute-done | bytes 786464 | tf_op jit(solution)/shard_map/ppermute | solution.py:337
  312.7 4.6 attend_grad.12
  324.6 4.6 attend_grad.15
  335.8 4.6 attend_grad.14
  359.0 4.8 attend_grad.13
  372.3 60.0 %psum.7 = f32[9216]{0:T(1024)S(1)} all-reduce(f32[9216]{0:T(1024)S(1)} %constant_dynamic-update-slice_fusion), channel_id=1, replica_groups=mesh['section'=2,'dp'=4,'tensor'=4] {'dp','tensor'}, use_global_device_ids=true, to_apply=%region_36.37 | all-reduce | flops 9216 | bytes 73728 | tf_op jit(solution)/shard_map/psum | solution.py:347
  464.3 16.3 %collective-permute-done.25 = bf16[768,768]{0,1:T(8,128)(2,1)S(1)} collective-permute-done((bf16[768,768]{0,1:T(8,128)(2,1)S(1)}, bf16[768,768]{0,1:T(8,128)(2,1)S(1)}, u32[]{:S(2)}, u32[]{:S(2)}) %collective-permute-start.25) | collective-permute-done | bytes 1179680 | tf_op jit(solution)/shard_map/ppermute | solution.py:141
  481.7 24.2 %collective-permute-done.31 = bf16[768,768]{1,0:T(8,128)(2,1)S(1)} collective-permute-done((bf16[768,768]{1,0:T(8,128)(2,1)S(1)}, bf16[768,768]{1,0:T(8,128)(2,1)S(1)}, u32[]{:S(2)}, u32[]{:S(2)}) %collective-permute-start.31) | collective-permute-done | bytes 1179680 | tf_op jit(solution)/shard_map/ppermute | solution.py:141
  507.2 3.8 collective-permute-start.34
  511.0 19.8 %collective-permute-done.37 = bf16[768,768]{1,0:T(8,128)(2,1)S(1)} collective-permute-done((bf16[768,768]{1,0:T(8,128)(2,1)S(1)}, bf16[768,768]{1,0:T(8,128)(2,1)S(1)}, u32[]{:S(2)}, u32[]{:S(2)}) %collective-permute-start.37) | collective-permute-done | bytes 1179680 | tf_op jit(solution)/shard_map/ppermute | solution.py:141
  533.6 3.8 collective-permute-start.40
  540.8 8.5 %collective-permute-done.33 = bf16[192,768]{1,0:T(8,128)(2,1)} collective-permute-done((bf16[192,768]{1,0:T(8,128)(2,1)}, bf16[192,768]{1,0:T(8,128)(2,1)}, u32[]{:S(2)}, u32[]{:S(2)}) %collective-permute-start.33) | collective-permute-done | bytes 294944 | tf_op jit(solution)/shard_map/ppermute | solution.py:180
  551.3 4.2 collective-permute-done.40
  555.5 19.0 %collective-permute-done.39 = bf16[192,768]{1,0:T(8,128)(2,1)} collective-permute-done((bf16[192,768]{1,0:T(8,128)(2,1)}, bf16[192,768]{1,0:T(8,128)(2,1)}, u32[]{:S(2)}, u32[]{:S(2)}) %collective-permute-start.39) | collective-permute-done | bytes 294944 | tf_op jit(solution)/shard_map/ppermute | solution.py:180
  (559 shorter events, 233.1 us)
Async XLA Ops:
  7.6 42.7 %collective-permute-start.5 = (bf16[768,768]{0,1:T(8,128)(2,1)}, bf16[768,768]{0,1:T(8,128)(2,1)S(1)}, u32[]{:S(2)}, u32[]{:S(2)}) collective-permute-start(bf16[768,768]{0,1:T(8,128)(2,1)} %pad_maximum_fusion), channel_id=1, source_target_pairs={{0,2},{1,3},{2,0},{3,1},{4,6},{5,7},{6,4},{7,5},{8,10},{9,11},{10,... | collective-permute-start | bytes 3538952 | tf_op jit(solution)/shard_map/ppermute | solution.py:141
  7.6 62.7 %collective-permute-start.3 = (bf16[768,768]{0,1:T(8,128)(2,1)}, bf16[768,768]{0,1:T(8,128)(2,1)}, u32[]{:S(2)}, u32[]{:S(2)}) collective-permute-start(bf16[768,768]{0,1:T(8,128)(2,1)} %pad_maximum_fusion), channel_id=1, source_target_pairs={{0,1},{1,0},{2,3},{3,2},{4,5},{5,4},{6,7},{7,6},{8,9},{9,8},{10,11... | collective-permute-start | bytes 3538952 | tf_op jit(solution)/shard_map/ppermute | solution.py:141
  9.4 30.6 %collective-permute-start = (bf16[128,768]{1,0:T(8,128)(2,1)S(1)}, bf16[128,768]{1,0:T(8,128)(2,1)S(1)}, u32[]{:S(2)}, u32[]{:S(2)}) collective-permute-start(bf16[128,768]{1,0:T(8,128)(2,1)S(1)} %get-tuple-element.126), channel_id=1, source_target_pairs={{0,3},{1,2},{2,1},{3,0},{4,7},{5,6},{6,5},{7,4},{8,11},{9,10},{10,... | collective-permute-start | bytes 589832 | tf_op jit(solution)/shard_map/ppermute | solution.py:141
  13.0 31.9 %collective-permute-start.1 = (bf16[128,768]{1,0:T(8,128)(2,1)S(1)}, bf16[128,768]{1,0:T(8,128)(2,1)S(1)}, u32[]{:S(2)}, u32[]{:S(2)}) collective-permute-start(bf16[128,768]{1,0:T(8,128)(2,1)S(1)} %get-tuple-element.125), channel_id=1, source_target_pairs={{0,2},{1,3},{2,0},{3,1},{4,6},{5,7},{6,4},{7,5},{8,10},{9,11},{10,... | collective-permute-start | bytes 589832 | tf_op jit(solution)/shard_map/ppermute | solution.py:141
  14.5 30.5 %collective-permute-start.2 = (bf16[128,768]{1,0:T(8,128)(2,1)S(1)}, bf16[128,768]{1,0:T(8,128)(2,1)S(1)}, u32[]{:S(2)}, u32[]{:S(2)}) collective-permute-start(bf16[128,768]{1,0:T(8,128)(2,1)S(1)} %get-tuple-element.124), channel_id=1, source_target_pairs={{0,1},{1,0},{2,3},{3,2},{4,5},{5,4},{6,7},{7,6},{8,9},{9,8},{10,11... | collective-permute-start | bytes 589832 | tf_op jit(solution)/shard_map/ppermute | solution.py:141
  40.0 30.4 %collective-permute-start.12 = (bf16[768,768]{1,0:T(8,128)(2,1)}, bf16[768,768]{1,0:T(8,128)(2,1)}, u32[]{:S(2)}, u32[]{:S(2)}) collective-permute-start(bf16[768,768]{1,0:T(8,128)(2,1)} %bitcast.206), channel_id=1, source_target_pairs={{0,2},{1,3},{2,0},{3,1},{4,6},{5,7},{6,4},{7,5},{8,10},{9,11},{10,... | collective-permute-start | bytes 3538952 | tf_op jit(solution)/shard_map/ppermute | solution.py:141
  45.0 71.1 %collective-permute-start.10 = (bf16[768,768]{1,0:T(8,128)(2,1)}, bf16[768,768]{1,0:T(8,128)(2,1)}, u32[]{:S(2)}, u32[]{:S(2)}) collective-permute-start(bf16[768,768]{1,0:T(8,128)(2,1)} %bitcast.207), channel_id=1, source_target_pairs={{0,1},{1,0},{2,3},{3,2},{4,5},{5,4},{6,7},{7,6},{8,9},{9,8},{10,11... | collective-permute-start | bytes 3538952 | tf_op jit(solution)/shard_map/ppermute | solution.py:141
  45.0 50.3 %collective-permute-start.11 = (bf16[768,768]{1,0:T(8,128)(2,1)}, bf16[768,768]{1,0:T(8,128)(2,1)}, u32[]{:S(2)}, u32[]{:S(2)}) collective-permute-start(bf16[768,768]{1,0:T(8,128)(2,1)} %bitcast.12), channel_id=1, source_target_pairs={{0,2},{1,3},{2,0},{3,1},{4,6},{5,7},{6,4},{7,5},{8,10},{9,11},{10,... | collective-permute-start | bytes 3538952 | tf_op jit(solution)/shard_map/ppermute | solution.py:141
  50.2 51.6 %collective-permute-start.7 = (bf16[768,768]{0,1:T(8,128)(2,1)S(1)}, bf16[768,768]{0,1:T(8,128)(2,1)S(1)}, u32[]{:S(2)}, u32[]{:S(2)}) collective-permute-start(bf16[768,768]{0,1:T(8,128)(2,1)S(1)} %collective-permute-done.5), channel_id=1, source_target_pairs={{0,1},{1,0},{2,3},{3,2},{4,5},{5,4},{6,7},{7,6},{8,9},{9,8},{10,11... | collective-permute-start | bytes 3538952 | tf_op jit(solution)/shard_map/ppermute | solution.py:141
  70.3 45.7 %collective-permute-start.9 = (bf16[768,768]{1,0:T(8,128)(2,1)}, bf16[768,768]{1,0:T(8,128)(2,1)}, u32[]{:S(2)}, u32[]{:S(2)}) collective-permute-start(bf16[768,768]{1,0:T(8,128)(2,1)} %bitcast.12), channel_id=1, source_target_pairs={{0,1},{1,0},{2,3},{3,2},{4,5},{5,4},{6,7},{7,6},{8,9},{9,8},{10,11... | collective-permute-start | bytes 3538952 | tf_op jit(solution)/shard_map/ppermute | solution.py:141
  70.3 50.1 %collective-permute-start.14 = (bf16[768,768]{1,0:T(8,128)(2,1)}, bf16[768,768]{1,0:T(8,128)(2,1)}, u32[]{:S(2)}, u32[]{:S(2)}) collective-permute-start(bf16[768,768]{1,0:T(8,128)(2,1)} %collective-permute-done.12), channel_id=1, source_target_pairs={{0,1},{1,0},{2,3},{3,2},{4,5},{5,4},{6,7},{7,6},{8,9},{9,8},{10,11... | collective-permute-start | bytes 3538952 | tf_op jit(solution)/shard_map/ppermute | solution.py:141
  95.2 25.2 %collective-permute-start.13 = (bf16[768,768]{1,0:T(8,128)(2,1)}, bf16[768,768]{1,0:T(8,128)(2,1)}, u32[]{:S(2)}, u32[]{:S(2)}) collective-permute-start(bf16[768,768]{1,0:T(8,128)(2,1)} %collective-permute-done.11), channel_id=1, source_target_pairs={{0,1},{1,0},{2,3},{3,2},{4,5},{5,4},{6,7},{7,6},{8,9},{9,8},{10,11... | collective-permute-start | bytes 3538952 | tf_op jit(solution)/shard_map/ppermute | solution.py:141
  126.1 21.2 %collective-permute-start.15 = (bf16[512,768]{1,0:T(8,128)(2,1)}, bf16[512,768]{1,0:T(8,128)(2,1)S(1)}, u32[]{:S(2)}, u32[]{:S(2)}) collective-permute-start(bf16[512,768]{1,0:T(8,128)(2,1)} %multiply_convert_fusion.5), channel_id=1, source_target_pairs={{0,16},{1,17},{2,18},{3,19},{4,20},{5,21},{6,22},{7,23},{8,24},{9,... | collective-permute-start | bytes 2359304 | tf_op jit(solution)/shard_map/ppermute | solution.py:332
  259.4 21.2 %collective-permute-start.19 = (bf16[512,768]{1,0:T(8,128)(2,1)S(1)}, bf16[512,768]{1,0:T(8,128)(2,1)S(1)}, u32[]{:S(2)}, u32[]{:S(2)}) collective-permute-start(bf16[512,768]{1,0:T(8,128)(2,1)S(1)} %add_convert_fusion.7), channel_id=1, source_target_pairs={{16,0},{17,1},{18,2},{19,3},{20,4},{21,5},{22,6},{23,7},{24,8},{25... | collective-permute-start | bytes 2359304 | tf_op jit(solution)/shard_map/ppermute | solution.py:337
  269.5 173.5 %collective-permute-start.17 = (bf16[128,768]{1,0:T(8,128)(2,1)}, bf16[128,768]{1,0:T(8,128)(2,1)}, u32[]{:S(2)}, u32[]{:S(2)}) collective-permute-start(bf16[128,768]{1,0:T(8,128)(2,1)} %get-tuple-element.122), channel_id=1, source_target_pairs={{0,2},{1,3},{2,0},{3,1},{4,6},{5,7},{6,4},{7,5},{8,10},{9,11},{10,... | collective-permute-start | bytes 589832 | tf_op jit(solution)/shard_map/ppermute | solution.py:141
  270.1 173.6 %collective-permute-start.16 = (bf16[128,768]{1,0:T(8,128)(2,1)}, bf16[128,768]{1,0:T(8,128)(2,1)}, u32[]{:S(2)}, u32[]{:S(2)}) collective-permute-start(bf16[128,768]{1,0:T(8,128)(2,1)} %get-tuple-element.123), channel_id=1, source_target_pairs={{0,3},{1,2},{2,1},{3,0},{4,7},{5,6},{6,5},{7,4},{8,11},{9,10},{10,... | collective-permute-start | bytes 589832 | tf_op jit(solution)/shard_map/ppermute | solution.py:141
  434.7 16.2 %collective-permute-start.30 = (bf16[768,768]{1,0:T(8,128)(2,1)}, bf16[768,768]{1,0:T(8,128)(2,1)}, u32[]{:S(2)}, u32[]{:S(2)}) collective-permute-start(bf16[768,768]{1,0:T(8,128)(2,1)} %convolution_convert_fusion.2), channel_id=1, source_target_pairs={{0,1},{1,0},{2,3},{3,2},{4,5},{5,4},{6,7},{7,6},{8,9},{9,8},{10,11... | collective-permute-start | bytes 3538952 | tf_op jit(solution)/shard_map/ppermute | solution.py:141
  435.2 22.9 %collective-permute-start.36 = (bf16[768,768]{1,0:T(8,128)(2,1)}, bf16[768,768]{1,0:T(8,128)(2,1)}, u32[]{:S(2)}, u32[]{:S(2)}) collective-permute-start(bf16[768,768]{1,0:T(8,128)(2,1)} %convolution_convert_fusion), channel_id=1, source_target_pairs={{0,1},{1,0},{2,3},{3,2},{4,5},{5,4},{6,7},{7,6},{8,9},{9,8},{10,11... | collective-permute-start | bytes 3538952 | tf_op jit(solution)/shard_map/ppermute | solution.py:141
  443.6 17.9 %collective-permute-start.23 = (bf16[768,768]{0,1:T(8,128)(2,1)S(1)}, bf16[768,768]{0,1:T(8,128)(2,1)S(1)}, u32[]{:S(2)}, u32[]{:S(2)}) collective-permute-start(bf16[768,768]{0,1:T(8,128)(2,1)S(1)} %pad_maximum_fusion.1), channel_id=1, source_target_pairs={{0,1},{1,0},{2,3},{3,2},{4,5},{5,4},{6,7},{7,6},{8,9},{9,8},{10,11... | collective-permute-start | bytes 3538952 | tf_op jit(solution)/shard_map/ppermute | solution.py:141
  450.9 29.7 %collective-permute-start.25 = (bf16[768,768]{0,1:T(8,128)(2,1)S(1)}, bf16[768,768]{0,1:T(8,128)(2,1)S(1)}, u32[]{:S(2)}, u32[]{:S(2)}) collective-permute-start(bf16[768,768]{0,1:T(8,128)(2,1)S(1)} %fusion.7), channel_id=1, source_target_pairs={{0,2},{1,3},{2,0},{3,1},{4,6},{5,7},{6,4},{7,5},{8,10},{9,11},{10,... | collective-permute-start | bytes 3538952 | tf_op jit(solution)/shard_map/ppermute | solution.py:141
  455.3 26.3 %collective-permute-start.29 = (bf16[768,768]{1,0:T(8,128)(2,1)S(1)}, bf16[768,768]{1,0:T(8,128)(2,1)S(1)}, u32[]{:S(2)}, u32[]{:S(2)}) collective-permute-start(bf16[768,768]{1,0:T(8,128)(2,1)S(1)} %copy-done.140), channel_id=1, source_target_pairs={{0,1},{1,0},{2,3},{3,2},{4,5},{5,4},{6,7},{7,6},{8,9},{9,8},{10,11... | collective-permute-start | bytes 3538952 | tf_op jit(solution)/shard_map/ppermute | solution.py:141
  455.3 50.5 %collective-permute-start.31 = (bf16[768,768]{1,0:T(8,128)(2,1)S(1)}, bf16[768,768]{1,0:T(8,128)(2,1)S(1)}, u32[]{:S(2)}, u32[]{:S(2)}) collective-permute-start(bf16[768,768]{1,0:T(8,128)(2,1)S(1)} %add_convert_fusion.1), channel_id=1, source_target_pairs={{0,2},{1,3},{2,0},{3,1},{4,6},{5,7},{6,4},{7,5},{8,10},{9,11},{10,... | collective-permute-start | bytes 3538952 | tf_op jit(solution)/shard_map/ppermute | solution.py:141
  458.7 48.5 %collective-permute-start.35 = (bf16[768,768]{1,0:T(8,128)(2,1)S(1)}, bf16[768,768]{1,0:T(8,128)(2,1)S(1)}, u32[]{:S(2)}, u32[]{:S(2)}) collective-permute-start(bf16[768,768]{1,0:T(8,128)(2,1)S(1)} %copy-done.139), channel_id=1, source_target_pairs={{0,1},{1,0},{2,3},{3,2},{4,5},{5,4},{6,7},{7,6},{8,9},{9,8},{10,11... | collective-permute-start | bytes 3538952 | tf_op jit(solution)/shard_map/ppermute | solution.py:141
  461.6 69.3 %collective-permute-start.37 = (bf16[768,768]{1,0:T(8,128)(2,1)S(1)}, bf16[768,768]{1,0:T(8,128)(2,1)S(1)}, u32[]{:S(2)}, u32[]{:S(2)}) collective-permute-start(bf16[768,768]{1,0:T(8,128)(2,1)S(1)} %add_convert_fusion), channel_id=1, source_target_pairs={{0,2},{1,3},{2,0},{3,1},{4,6},{5,7},{6,4},{7,5},{8,10},{9,11},{10,... | collective-permute-start | bytes 3538952 | tf_op jit(solution)/shard_map/ppermute | solution.py:141
  481.6 52.0 %collective-permute-start.28 = (bf16[192,768]{0,1:T(8,128)(2,1)S(1)}, bf16[192,768]{0,1:T(8,128)(2,1)S(1)}, u32[]{:S(2)}, u32[]{:S(2)}) collective-permute-start(bf16[192,768]{0,1:T(8,128)(2,1)S(1)} %get-tuple-element.116), channel_id=1, source_target_pairs={{0,12},{4,0},{8,4},{12,8},{1,13},{5,1},{9,5},{13,9},{2,14},{6,2},{... | collective-permute-start | bytes 884744 | tf_op jit(solution)/shard_map/ppermute | solution.py:180
  481.6 52.0 %collective-permute-start.27 = (bf16[192,768]{0,1:T(8,128)(2,1)S(1)}, bf16[192,768]{0,1:T(8,128)(2,1)S(1)}, u32[]{:S(2)}, u32[]{:S(2)}) collective-permute-start(bf16[192,768]{0,1:T(8,128)(2,1)S(1)} %get-tuple-element.117), channel_id=1, source_target_pairs={{0,8},{4,12},{8,0},{12,4},{1,9},{5,13},{9,1},{13,5},{2,10},{6,14},... | collective-permute-start | bytes 884744 | tf_op jit(solution)/shard_map/ppermute | solution.py:180
  505.9 31.6 %collective-permute-start.26 = (bf16[192,768]{0,1:T(8,128)(2,1)S(1)}, bf16[192,768]{0,1:T(8,128)(2,1)S(1)}, u32[]{:S(2)}, u32[]{:S(2)}) collective-permute-start(bf16[192,768]{0,1:T(8,128)(2,1)S(1)} %get-tuple-element.115), channel_id=1, source_target_pairs={{0,4},{4,8},{8,12},{12,0},{1,5},{5,9},{9,13},{13,1},{2,6},{6,10},{... | collective-permute-start | bytes 884744 | tf_op jit(solution)/shard_map/ppermute | solution.py:180
  507.2 31.6 %collective-permute-start.34 = (bf16[192,768]{1,0:T(8,128)(2,1)S(1)}, bf16[192,768]{1,0:T(8,128)(2,1)S(1)}, u32[]{:S(2)}, u32[]{:S(2)}) collective-permute-start(bf16[192,768]{1,0:T(8,128)(2,1)S(1)} %get-tuple-element.113), channel_id=1, source_target_pairs={{0,12},{4,0},{8,4},{12,8},{1,13},{5,1},{9,5},{13,9},{2,14},{6,2},{... | collective-permute-start | bytes 884744 | tf_op jit(solution)/shard_map/ppermute | solution.py:180
  530.9 18.4 %collective-permute-start.33 = (bf16[192,768]{1,0:T(8,128)(2,1)}, bf16[192,768]{1,0:T(8,128)(2,1)}, u32[]{:S(2)}, u32[]{:S(2)}) collective-permute-start(bf16[192,768]{1,0:T(8,128)(2,1)} %get-tuple-element.114), channel_id=1, source_target_pairs={{0,8},{4,12},{8,0},{12,4},{1,9},{5,13},{9,1},{13,5},{2,10},{6,14},... | collective-permute-start | bytes 884744 | tf_op jit(solution)/shard_map/ppermute | solution.py:180
  533.6 21.8 %collective-permute-start.40 = (bf16[192,768]{1,0:T(8,128)(2,1)}, bf16[192,768]{1,0:T(8,128)(2,1)}, u32[]{:S(2)}, u32[]{:S(2)}) collective-permute-start(bf16[192,768]{1,0:T(8,128)(2,1)} %get-tuple-element.110), channel_id=1, source_target_pairs={{0,12},{4,0},{8,4},{12,8},{1,13},{5,1},{9,5},{13,9},{2,14},{6,2},{... | collective-permute-start | bytes 884744 | tf_op jit(solution)/shard_map/ppermute | solution.py:180
  537.4 37.0 %collective-permute-start.39 = (bf16[192,768]{1,0:T(8,128)(2,1)}, bf16[192,768]{1,0:T(8,128)(2,1)}, u32[]{:S(2)}, u32[]{:S(2)}) collective-permute-start(bf16[192,768]{1,0:T(8,128)(2,1)} %get-tuple-element.111), channel_id=1, source_target_pairs={{0,8},{4,12},{8,0},{12,4},{1,9},{5,13},{9,1},{13,5},{2,10},{6,14},... | collective-permute-start | bytes 884744 | tf_op jit(solution)/shard_map/ppermute | solution.py:180
  538.9 35.6 %collective-permute-start.38 = (bf16[192,768]{1,0:T(8,128)(2,1)}, bf16[192,768]{1,0:T(8,128)(2,1)}, u32[]{:S(2)}, u32[]{:S(2)}) collective-permute-start(bf16[192,768]{1,0:T(8,128)(2,1)} %get-tuple-element.109), channel_id=1, source_target_pairs={{0,4},{4,8},{8,12},{12,0},{1,5},{5,9},{9,13},{13,1},{2,6},{6,10},{... | collective-permute-start | bytes 884744 | tf_op jit(solution)/shard_map/ppermute | solution.py:180
  (160 other events, 2218.2 us)
